TPU v7x, 32 devices: a whole 2x2x4 slice. The times are simulated.
32 devices in a mesh: row: 8 (over y, x, core), col: 4 (over z).
Axes of the slice: x: 2, y: 2, z: 4, core: 2. Of those that a mesh axis runs over, the one named last changes fastest.
Arguments:
- counts: int32 [8, 4, 6, 8, 128, 128], P('row', 'col'), may hold values from 0 to 5
- block_coords: int32 [3, 8, 4, 6], P(None, 'row', 'col'), may hold values from 0 to 127, as said below
- block_count: int32 [8, 4], P('row', 'col'), may hold values from 1 to 6, as said below
- factor_a: float32 [16384, 128], P(('row', 'col')), may hold values from -0.6 to 0.6
- factor_b: float32 [8192, 128], P(('col', 'row')), may hold values from -0.6 to 0.6
- factor_c: float32 [1024, 128], replicated, may hold values from -0.6 to 0.6
Outputs:
- updated_a: float32 [16384, 128], P(('row', 'col'))
- updated_b: float32 [8192, 128], P(('col', 'row'))
Inputs may be any that keep to these rules, and one draw needn't show every extreme that they name: `block_coords`: the slots of one cell name distinct blocks; the first index is below 16, the second below 16, the third below 128. `block_count`: at least one cell has all 6 slots live in every draw.
All inputs are finite; a program needn't handle non-finite values.
Results may differ from a plain program's by a relative error of at most 0.0003.
Values sent between devices are 32-bit elements; how exact they have to be, the bound alone decides.
A program may use at most 64 MiB of HBM per device.

v0:
```python
import jax
import jax.numpy as jnp
from jax import lax
from jax.sharding import PartitionSpec as P

STEPS = 2


step_rate = 0.004
highest = lax.Precision.HIGHEST


def block_gradient(piece_a, piece_b, piece_c, observed, valid_flag):
    depth = piece_c.shape[0]
    side = piece_a.shape[0]
    rank = piece_a.shape[1]
    scaled_a = (piece_c[:, None, :] * piece_a[None, :, :]).reshape(depth * side, rank)
    model = jnp.dot(scaled_a, piece_b.T, precision=highest, preferred_element_type=jnp.float32)
    residual = (
        jnp.exp(model) - observed.reshape(depth * side, side).astype(jnp.float32)
    ) * valid_flag
    scaled_b = piece_c[:, None, :] * piece_b[None, :, :]
    grad_a = jnp.einsum(
        "kab,kbr->ar", residual.reshape(depth, side, side), scaled_b, precision=highest
    )
    grad_b = jnp.dot(residual.T, scaled_a, precision=highest, preferred_element_type=jnp.float32)
    return (grad_a, grad_b)


def local_gradients(band_a, band_b, factor_c, counts, block_coords, block_count):
    depth = counts.shape[3]
    side = counts.shape[4]
    limit = block_count[0, 0]

    def visit_slot(partial_value, slot_index):
        grad_a, grad_b = partial_value
        start_a = block_coords[0, 0, 0, slot_index] * side
        start_b = block_coords[1, 0, 0, slot_index] * side
        start_c = block_coords[2, 0, 0, slot_index] * depth
        valid_flag = (slot_index < limit).astype(jnp.float32)
        piece_a = lax.dynamic_slice_in_dim(band_a, start_a, side, 0)
        piece_b = lax.dynamic_slice_in_dim(band_b, start_b, side, 0)
        piece_c = lax.dynamic_slice_in_dim(factor_c, start_c, depth, 0)
        observed = counts[0, 0, slot_index]
        block_a, block_b = block_gradient(piece_a, piece_b, piece_c, observed, valid_flag)
        old_a = lax.dynamic_slice_in_dim(grad_a, start_a, side, 0)
        old_b = lax.dynamic_slice_in_dim(grad_b, start_b, side, 0)
        grad_a = lax.dynamic_update_slice_in_dim(grad_a, old_a + block_a, start_a, 0)
        grad_b = lax.dynamic_update_slice_in_dim(grad_b, old_b + block_b, start_b, 0)
        return ((grad_a, grad_b), None)

    start = (jnp.zeros_like(band_a), jnp.zeros_like(band_b))
    result = lax.fori_loop(
        0, limit, lambda slot_index, partial_value: visit_slot(partial_value, slot_index)[0], start
    )
    return result


def local(counts, block_coords, block_count, factor_a, factor_b, factor_c):
    for step_index in range(STEPS):
        band_a = lax.all_gather(factor_a, "col", axis=0, tiled=True)
        band_b = lax.all_gather(factor_b, "row", axis=0, tiled=True)
        grad_a, grad_b = local_gradients(
            band_a, band_b, factor_c, counts, block_coords, block_count
        )
        share_a = lax.psum_scatter(grad_a, "col", scatter_dimension=0, tiled=True)
        share_b = lax.psum_scatter(grad_b, "row", scatter_dimension=0, tiled=True)
        factor_a = factor_a - step_rate * share_a
        factor_b = factor_b - step_rate * share_b
    return (factor_a, factor_b)


def solution(mesh):
    return jax.shard_map(
        local,
        mesh=mesh,
        in_specs=(
            P("row", "col", None, None, None, None),
            P(None, "row", "col", None),
            P("row", "col"),
            P(("row", "col"), None),
            P(("col", "row"), None),
            P(),
        ),
        out_specs=(P(("row", "col"), None), P(("col", "row"), None)),
        check_vma=False,
    )
```

profile of v0, /device:TPU:0, one launch (start us, length us, event | category | flops | bytes accessed | tf_op | source)
XLA Modules:
  0.0 372.1 jit_solution(14992824888920372945)
XLA Ops:
  7.9 0.7 all-gather.7.cloned.1.call-update
  8.7 31.5 %all-gather.5.cloned.1.call-done = f32[2048,128]{1,0:T(8,128)} async-done(((f32[512,128]{1,0:T(8,128)}), f32[2048,128]{1,0:T(8,128)}) %all-gather.5.cloned.1.call-update) | async-done | bytes 1048592 | tf_op jit(solution)/shard_map/all_gather | solution.py:61
  40.2 24.9 %all-gather.7.cloned.1.call-done = f32[2048,128]{1,0:T(8,128)} async-done(((f32[256,128]{1,0:T(8,128)}), f32[2048,128]{1,0:T(8,128)}) %all-gather.7.cloned.1.call-update) | async-done | bytes 1048592 | tf_op jit(solution)/shard_map/all_gather | solution.py:62
  65.3 39.0 %while.24 = (s32[]{:T(128)}, f32[2048,128]{1,0:T(8,128)S(1)}, f32[2048,128]{1,0:T(8,128)S(1)}, s32[]{:T(128)}, s32[3,1,1,6]{3,2,1,0:T(1,128)}, /*index=5*/f32[10...) while((s32[]{:T(128)}, f32[2048,128]{1,0:T(8,128)S(1)}, ...), condition=%wide.region_1.0_spmd, body=%wide.region_0.0_spmd.sunk | while | flops 604667904 | bytes 5456263 | solution.py:53
  66.0 1.3 constant_dynamic-slice_fusion.18
  68.6 0.9 constant_dynamic-slice_fusion.19
  70.1 0.7 constant_dynamic-slice_fusion.20
  70.9 1.1 dynamic-slice_convert_fusion.4
  73.2 1.0 fusion.52
  75.6 1.3 constant_dynamic-slice_fusion.18
  78.2 0.9 constant_dynamic-slice_fusion.19
  79.7 0.7 constant_dynamic-slice_fusion.20
  80.4 1.1 dynamic-slice_convert_fusion.4
  82.8 1.0 fusion.52
  85.2 1.3 constant_dynamic-slice_fusion.18
  87.8 0.9 constant_dynamic-slice_fusion.19
  89.3 0.7 constant_dynamic-slice_fusion.20
  90.0 1.1 dynamic-slice_convert_fusion.4
  92.4 1.0 fusion.52
  94.7 1.3 constant_dynamic-slice_fusion.18
  97.3 0.9 constant_dynamic-slice_fusion.19
  99.6 1.1 dynamic-slice_convert_fusion.4
  101.9 1.0 fusion.52
  104.3 1.0 copy-done.3
  106.0 54.6 %reduce-scatter.7.cloned.1.call-done = f32[256,128]{1,0:T(8,128)} async-done(((f32[2048,128]{1,0:T(8,128)}), f32[256,128]{1,0:T(8,128)}) %reduce-scatter.7.cloned.1.call-update) | async-done | bytes 131088 | tf_op jit(solution)/shard_map/reduce_scatter | solution.py:67
  160.5 1.6 multiply_subtract_fusion.3
  162.2 27.6 %reduce-scatter.5.cloned.1.call-done = f32[512,128]{1,0:T(8,128)} async-done(((f32[2048,128]{1,0:T(8,128)}), f32[512,128]{1,0:T(8,128)}) %reduce-scatter.5.cloned.1.call-update) | async-done | bytes 262160 | tf_op jit(solution)/shard_map/reduce_scatter | solution.py:66
  189.8 1.7 multiply_subtract_fusion.1
  191.6 22.9 %all-gather.11.cloned.1.call-done = f32[2048,128]{1,0:T(8,128)} async-done(((f32[256,128]{1,0:T(8,128)}), f32[2048,128]{1,0:T(8,128)}) %all-gather.11.cloned.1.call-update) | async-done | bytes 1048592 | tf_op jit(solution)/shard_map/all_gather | solution.py:62
  214.5 30.0 %all-gather.9.cloned.1.call-done = f32[2048,128]{1,0:T(8,128)} async-done(((f32[512,128]{1,0:T(8,128)}), f32[2048,128]{1,0:T(8,128)}) %all-gather.9.cloned.1.call-update) | async-done | bytes 1048592 | tf_op jit(solution)/shard_map/all_gather | solution.py:61
  244.7 36.2 %while.25 = (s32[]{:T(128)}, f32[2048,128]{1,0:T(8,128)S(1)}, f32[2048,128]{1,0:T(8,128)S(1)}, s32[]{:T(128)}, s32[3,1,1,6]{3,2,1,0:T(1,128)S(1)}, /*index=5*/f3...) while((s32[]{:T(128)}, f32[2048,128]{1,0:T(8,128)S(1)}, ...), condition=%wide.region_5.0_spmd, body=%wide.region_4.0_spmd.sunk | while | flops 604667904 | bytes 5456263 | solution.py:53
  247.3 0.9 constant_dynamic-slice_fusion.22
  249.5 1.1 dynamic-slice_convert_fusion.5
  251.9 1.0 fusion.61
  256.1 0.9 constant_dynamic-slice_fusion.22
  258.4 1.1 dynamic-slice_convert_fusion.5
  260.7 1.0 fusion.61
  265.0 0.9 constant_dynamic-slice_fusion.22
  267.3 1.1 dynamic-slice_convert_fusion.5
  269.6 1.0 fusion.61
  273.9 0.9 constant_dynamic-slice_fusion.22
  276.1 1.1 dynamic-slice_convert_fusion.5
  278.5 1.0 fusion.61
  280.9 0.9 copy-done.1
  282.6 51.4 %reduce-scatter.11.cloned.1.call-done = f32[256,128]{1,0:T(8,128)} async-done(((f32[2048,128]{1,0:T(8,128)}), f32[256,128]{1,0:T(8,128)}) %reduce-scatter.11.cloned.1.call-update) | async-done | bytes 131088 | tf_op jit(solution)/shard_map/reduce_scatter | solution.py:67
  334.0 1.6 multiply_subtract_fusion.2
  335.6 27.9 %reduce-scatter.9.cloned.1.call-done = f32[512,128]{1,0:T(8,128)} async-done(((f32[2048,128]{1,0:T(8,128)}), f32[512,128]{1,0:T(8,128)}) %reduce-scatter.9.cloned.1.call-update) | async-done | bytes 262160 | tf_op jit(solution)/shard_map/reduce_scatter | solution.py:66
  363.5 1.7 multiply_subtract_fusion
  (64 shorter events, 18.9 us)
Async XLA Ops:
  7.2 33.1 %all-gather.5.cloned.1.call-start = ((), (), s32[]{:S(2)}) async-start(), calls=%async_computation.4 | async-start | bytes 1310720 | tf_op jit(solution)/shard_map/all_gather | solution.py:61
  7.9 57.2 %all-gather.7.cloned.1.call-start = ((), (), s32[]{:S(2)}) async-start(), calls=%async_computation.5 | async-start | bytes 1179648 | tf_op jit(solution)/shard_map/all_gather | solution.py:62
  8.6 151.9 %reduce-scatter.7.cloned.1.call-start = ((), (), s32[]{:S(2)}) async-start(), calls=%async_computation.8 | async-start | bytes 1179648 | tf_op jit(solution)/shard_map/reduce_scatter | solution.py:67
  65.3 124.5 %copy-start.5 = (f32[512,128]{1,0:T(8,128)S(1)}, f32[512,128]{1,0:T(8,128)}, u32[]{:S(2)}) copy-start(f32[512,128]{1,0:T(8,128)} %param.13) | copy-start | bytes 786436
  104.3 1.0 copy-start.3
  104.3 1.3 copy-start.2
  104.3 140.3 %copy-start.6 = (s32[3,1,1,6]{3,2,1,0:T(1,128)S(1)}, s32[3,1,1,6]{3,2,1,0:T(1,128)}, u32[]{:S(2)}) copy-start(s32[3,1,1,6]{3,2,1,0:T(1,128)} %get-tuple-element.405) | copy-start | bytes 220
  105.3 84.5 %reduce-scatter.5.cloned.1.call-start = ((), (), s32[]{:S(2)}) async-start(), calls=%async_computation.6 | async-start | bytes 1310720 | tf_op jit(solution)/shard_map/reduce_scatter | solution.py:66
  105.9 108.6 %all-gather.11.cloned.1.call-start = ((), (), s32[]{:S(2)}) async-start(), calls=%async_computation.9 | async-start | bytes 1179648 | tf_op jit(solution)/shard_map/all_gather | solution.py:62
  162.2 82.3 %all-gather.9.cloned.1.call-start = ((), (), s32[]{:S(2)}) async-start(), calls=%async_computation.7 | async-start | bytes 1310720 | tf_op jit(solution)/shard_map/all_gather | solution.py:61
  191.5 142.4 %reduce-scatter.11.cloned.1.call-start = ((), (), s32[]{:S(2)}) async-start(), calls=%async_computation.11 | async-start | bytes 1179648 | tf_op jit(solution)/shard_map/reduce_scatter | solution.py:67
  244.7 118.9 %copy-start.4 = (f32[512,128]{1,0:T(8,128)S(1)}, f32[512,128]{1,0:T(8,128)}, u32[]{:S(2)}) copy-start(f32[512,128]{1,0:T(8,128)} %multiply_subtract_fusion.1) | copy-start | bytes 786436
  280.8 1.0 copy-start.1
  280.8 1.3 copy-start
  281.8 81.7 %reduce-scatter.9.cloned.1.call-start = ((), (), s32[]{:S(2)}) async-start(), calls=%async_computation.10 | async-start | bytes 1310720 | tf_op jit(solution)/shard_map/reduce_scatter | solution.py:66
Sparse Core Ops, SparseCore 0:
  9.6 30.6 all-gather.4
  42.1 22.9 all-gather.6
  105.4 55.0 reduce-scatter.6
  162.7 27.1 reduce-scatter.4
  192.3 22.1 all-gather.10
  216.5 27.9 all-gather.8
  281.9 51.9 reduce-scatter.10
  336.4 27.1 reduce-scatter.8
where the time goes:
time: 374 us; the launch traced here: 372 us
  waiting for transfers between devices  273 us (73%)
  loops' own time  27.5 us (7%)
  local copies, waits for them, and re-layouts  23.1 us (6%)
  matrix products  18.2 us (5%)
  other arithmetic  15.6 us (4%)
  between operations  14.2 us (4%)
    reduce_scatter x2, waiting for transfers between devices, local(): share_b = lax.psum_scatter(grad_b, 'row', scatter_dimension=0, tiled=True)  106 us
    all_gather x2, waiting for transfers between devices, local(): band_a = lax.all_gather(factor_a, 'col', axis=0, tiled=True)  61.6 us
    reduce_scatter x2, waiting for transfers between devices, local(): share_a = lax.psum_scatter(grad_a, 'col', scatter_dimension=0, tiled=True)  55.5 us
    all_gather x2, waiting for transfers between devices, local(): band_b = lax.all_gather(factor_b, 'row', axis=0, tiled=True)  47.8 us
    another operation x2, loops' own time, local_gradients(): lax.fori_loop(0, limit, lambda slot_index, partial_value: visit_slot(part...  27.5 us
    convert_element_type x8, other arithmetic, block_gradient(): observed.reshape(depth * side, side).astype(jnp.float32)  8.67 us
    dot_general x8, matrix products, block_gradient(): jnp.dot(residual.T, scaled_a, precision=highest, preferred_element_type=j...  8.21 us
    dynamic_slice x8, local copies, waits for them, and re-layouts, visit_slot(): start_b = block_coords[1, 0, 0, slot_index] * side  7.72 us
  transfers between devices with their start and end apart: 8, of which 8 were waited for; matrix products, arithmetic and copies ran while one was open for 1% of the time, Pallas kernels for 0%

commit v1 on v0

v1 whole, which is shorter than its diff:
```python
import functools

import jax
import jax.numpy as jnp
from jax import lax
from jax.experimental import pallas as pl
from jax.experimental.pallas import tpu as pltpu
from jax.sharding import PartitionSpec as P

STEPS = 2
step_rate = 0.004
MESH = pl.DeviceIdType.MESH


def split(x):
    high = x.astype(jnp.bfloat16)
    return high, (x - high.astype(jnp.float32)).astype(jnp.bfloat16)


def dot(x, y, dims):
    return lax.dot_general(x, y, (dims, ((), ())), preferred_element_type=jnp.float32)


def dot3(x, y, dims):
    return dot(x[0], y[0], dims) + (dot(x[0], y[1], dims) + dot(x[1], y[0], dims))


def kernel(n_row, n_col, coords, limit_ref, a_ref, b_ref, c_ref, counts_hbm, out_a, out_b,
           counts, band_a, band_b, cur_a, cur_b, raw_a, raw_b, tag_a, tag_b, acc_a, acc_b,
           counts_sem, ra_send, ra_recv, ga_send, ga_recv, gb_send, gb_recv, rb_send, rb_recv,
           ta_send, ta_recv, tb_send, tb_recv):
    r = lax.axis_index("row")
    c = lax.axis_index("col")
    own_a = a_ref.shape[0]
    own_b = b_ref.shape[0]
    side = a_ref.shape[1]
    slots = counts_hbm.shape[0]
    depth = c_ref.shape[1]
    chips = n_row // 2
    core = lax.rem(r, 2)
    partner = r + 1 - 2 * core
    limit = limit_ref[0, 0]

    def loop(n, body):
        lax.fori_loop(0, n, lambda i, carry: (body(i), carry)[1], 0)

    def row_peer(d):
        return lax.rem(r + d, n_row)

    def col_peer(d):
        return lax.rem(c + d, n_col)

    def chip_peer(d):
        return lax.rem(r + 2 * d, n_row)

    load_counts = [
        pltpu.make_async_copy(counts_hbm.at[s], counts.at[s], counts_sem.at[s]) for s in range(slots)
    ]
    for copy in load_counts:
        copy.start()

    barrier = pltpu.get_barrier_semaphore()
    loop(n_row - 1, lambda d: pl.semaphore_signal(
        barrier, inc=1, device_id=(row_peer(d + 1), c), device_id_type=MESH))
    loop(n_col - 1, lambda d: pl.semaphore_signal(
        barrier, inc=1, device_id=(r, col_peer(d + 1)), device_id_type=MESH))

    line = lax.broadcasted_iota(jnp.int32, tag_a.shape[1:], 0)
    mine_a = jnp.full(tag_a.shape[1:], -1.0, jnp.float32)
    mine_b = mine_a
    for s in range(slots):
        live = s < limit
        mine_a = jnp.where(line == s, jnp.where(live, coords[0, s], -1).astype(jnp.float32), mine_a)
        mine_b = jnp.where(line == s, jnp.where(live, coords[1, s], -1).astype(jnp.float32), mine_b)
    tag_a[c] = mine_a
    tag_b[r] = mine_b
    pl.semaphore_wait(barrier, n_row - 1 + n_col - 1)

    def chain(buf, send, recv, side_index, o, p, lead, src=None):
        to = c + 1 if side_index == 0 else c - 1
        place = buf.at[lead + (o, p)]
        return pltpu.make_async_remote_copy(
            src_ref=place if src is None else src,
            dst_ref=place,
            send_sem=send.at[lead + (side_index, o, p)],
            recv_sem=recv.at[lead + (o, p)],
            device_id=(r, to),
            device_id_type=MESH,
        )

    def across(buf, send, recv, o, p, lead, to, k, src=None):
        place = buf.at[lead + (o, p)]
        return pltpu.make_async_remote_copy(
            src_ref=place if src is None else src,
            dst_ref=place,
            send_sem=send.at[lead + (k, p)],
            recv_sem=recv.at[lead + (o, p)],
            device_id=(to, c),
            device_id_type=MESH,
        )

    def when(condition, body):
        pl.when(condition)(body)

    def chain_send(o, side_index, make, act):
        if side_index == 0:
            when(jnp.logical_and(o >= 0, jnp.logical_and(o <= c, c < n_col - 1)), lambda: act(make(0, o)))
        else:
            when(jnp.logical_and(o <= n_col - 1, jnp.logical_and(o >= c, c > 0)), lambda: act(make(1, o)))

    def gather_a(p):
        return lambda side_index, o: chain(band_a, ga_send, ga_recv, side_index, o, p, ())

    def gather_a_own(p):
        return lambda side_index, o: chain(band_a, ga_send, ga_recv, side_index, o, p, (), a_ref.at[p])

    def start(copy):
        copy.start()

    def wait_send(copy):
        copy.wait_send()

    for p in range(own_a):
        chain_send(c, 0, gather_a_own(p), start)
        chain_send(c, 1, gather_a_own(p), start)

    def gather_b(d, p):
        return across(band_b, gb_send, gb_recv, r, p, (), row_peer(d), d - 1, b_ref.at[p])

    def tag_copy_a(o, d):
        return pltpu.make_async_remote_copy(
            src_ref=tag_a.at[o], dst_ref=tag_a.at[o], send_sem=ta_send.at[d - 1], recv_sem=ta_recv.at[o],
            device_id=(r, col_peer(d)), device_id_type=MESH)

    def tag_copy_b(o, d):
        return pltpu.make_async_remote_copy(
            src_ref=tag_b.at[o], dst_ref=tag_b.at[o], send_sem=tb_send.at[d - 1], recv_sem=tb_recv.at[o],
            device_id=(row_peer(d), c), device_id_type=MESH)

    def send_b(d):
        for p in range(own_b):
            gather_b(d + 1, p).start()

    loop(n_row - 1, send_b)
    loop(n_col - 1, lambda d: tag_copy_a(c, d + 1).start())
    loop(n_row - 1, lambda d: tag_copy_b(r, d + 1).start())
    for p in range(own_a):
        band_a[c, p] = a_ref[p]
    for p in range(own_b):
        band_b[r, p] = b_ref[p]

    def pass_on(make, recv_wait, d):
        left, right = c - d, c + d

        def from_left():
            recv_wait(left)
            chain_send(left, 0, make, start)

        def from_right():
            recv_wait(right)
            chain_send(right, 1, make, start)

        when(left >= 0, from_left)
        when(right < n_col, from_right)

    def pass_a(d):
        for p in range(own_a):
            pass_on(gather_a(p), lambda o: chain(band_a, ga_send, ga_recv, 0, o, p, ()).wait_recv(), d + 1)

    loop(n_col - 1, pass_a)

    def receive_b(d):
        for p in range(own_b):
            across(band_b, gb_send, gb_recv, row_peer(d + 1), p, (), r, 0).wait_recv()

    loop(n_row - 1, receive_b)
    loop(n_col - 1, lambda d: tag_copy_a(col_peer(d + 1), 1).wait_recv())
    loop(n_row - 1, lambda d: tag_copy_b(row_peer(d + 1), 1).wait_recv())

    def first_pieces(s):
        ia = coords[0, s]
        ib = coords[1, s]
        cur_a[s] = band_a[ia // own_a, ia % own_a]
        cur_b[s] = band_b[ib // own_b, ib % own_b]

    loop(slots, first_pieces)

    def gradients(t, s):
        piece_a = cur_a[s]
        piece_b = cur_b[s]
        piece_c = c_ref[coords[2, s]]
        flag = jnp.where(s < limit, 1.0, 0.0).astype(jnp.float32)
        scaled = (piece_c[:, None, :] * piece_a[None, :, :]).reshape(depth * side, -1)
        scaled = split(scaled)
        split_b = split(piece_b)
        model = dot3(scaled, split_b, ((1,), (1,)))
        observed = counts[s].astype(jnp.float32)
        residual = split((jnp.exp(model) - observed) * flag)
        product = dot3(residual, split_b, ((1,), (0,)))
        grad_a = jnp.sum(product.reshape(depth, side, -1) * piece_c[:, None, :], axis=0)
        grad_b = dot3(residual, scaled, ((0,), (0,)))
        if t:
            grad_a = grad_a + raw_a[t - 1, c, s]
            grad_b = grad_b + raw_b[t - 1, r, s]
        raw_a[t, c, s] = grad_a
        raw_b[t, r, s] = grad_b

    def absorb(raw, tag, acc, ids, t, o):
        tags = tag[o]
        for i, block in enumerate(ids):
            match = [tags[s:s + 1, :] == block for s in range(slots)]
            total = acc[i]
            for s in range(slots):
                total = total + jnp.where(match[s], raw[t, o, s], 0.0)
            acc[i] = total

    def step(t):
        last = t == STEPS - 1

        def spread(s):
            make = lambda side_index, o: chain(raw_a, ra_send, ra_recv, side_index, o, s, (t,))
            chain_send(c, 0, make, start)
            chain_send(c, 1, make, start)
            across(raw_b, rb_send, rb_recv, r, s, (t,), partner, chips - 1).start()
            loop(chips - 1, lambda d: across(raw_b, rb_send, rb_recv, r, s, (t,), chip_peer(d + 1), d).start())

        def one(s):
            for k in range(slots):
                if t == 0:
                    when(s == k, load_counts[k].wait)
            gradients(t, s)
            spread(s)

        loop(slots, one)
        if last:
            ids_a = [(c * own_a + p).astype(jnp.float32) for p in range(own_a)]
            ids_b = [(r * own_b + p).astype(jnp.float32) for p in range(own_b)]
        else:
            ids_a = [coords[0, s].astype(jnp.float32) for s in range(slots)]
            ids_b = [coords[1, s].astype(jnp.float32) for s in range(slots)]
        acc_a[...] = jnp.zeros_like(acc_a)
        acc_b[...] = jnp.zeros_like(acc_b)
        take_a = lambda o: absorb(raw_a, tag_a, acc_a, ids_a, t, o)
        take_b = lambda o: absorb(raw_b, tag_b, acc_b, ids_b, t, o)

        def forward(d):
            def passing(s):
                make = lambda side_index, o: chain(raw_a, ra_send, ra_recv, side_index, o, s, (t,))
                pass_on(make, lambda o: make(0, o).wait_recv(), d)
                origin = chip_peer(d)

                def hand_over():
                    across(raw_b, rb_send, rb_recv, origin, s, (t,), r, 0).wait_recv()
                    across(raw_b, rb_send, rb_recv, origin, s, (t,), partner, chips - 1 + d).start()

                when(d < chips, hand_over)

            loop(slots, passing)

        def receive_partner(d):
            origin = lax.rem(partner + 2 * d, n_row)
            for s in range(slots):
                across(raw_b, rb_send, rb_recv, origin, s, (t,), r, 0).wait_recv()

        loop(max(n_col, chips) - 1, lambda d: forward(d + 1))
        loop(chips, receive_partner)
        loop(n_col, take_a)
        loop(n_row, take_b)
        if last:
            for p in range(own_a):
                out_a[p] = a_ref[p] - step_rate * acc_a[p]
            for p in range(own_b):
                out_b[p] = b_ref[p] - step_rate * acc_b[p]
        else:
            for s in range(slots):
                cur_a[s] = cur_a[s] - step_rate * acc_a[s]
                cur_b[s] = cur_b[s] - step_rate * acc_b[s]

    for t in range(STEPS):
        step(t)

    def sent_a(o):
        for side_index in range(2):
            for p in range(own_a):
                chain_send(o, side_index, gather_a(p), wait_send)
            for t in range(STEPS):
                def sent(s):
                    make = lambda k, origin: chain(raw_a, ra_send, ra_recv, k, origin, s, (t,))
                    chain_send(o, side_index, make, wait_send)

                loop(slots, sent)

    loop(n_col, sent_a)

    def sent_b(d):
        for p in range(own_b):
            gather_b(d + 1, p).wait_send()

    loop(n_row - 1, sent_b)
    loop(n_col - 1, lambda d: tag_copy_a(c, d + 1).wait_send())
    loop(n_row - 1, lambda d: tag_copy_b(r, d + 1).wait_send())
    for t in range(STEPS):
        def sent_raw_b(k):
            for s in range(slots):
                across(raw_b, rb_send, rb_recv, r, s, (t,), partner, k).wait_send()

        loop(2 * chips - 1, sent_raw_b)


def local(n_row, n_col, counts, block_coords, block_count, factor_a, factor_b, factor_c):
    slots, depth, side = counts.shape[2:5]
    rank = factor_a.shape[1]
    own_a = factor_a.shape[0] // side
    own_b = factor_b.shape[0] // side
    chips = n_row // 2
    lines = -(-slots // 8) * 8
    f32 = jnp.float32
    vmem = pl.BlockSpec(memory_space=pltpu.VMEM)
    smem = pl.BlockSpec(memory_space=pltpu.SMEM)
    dma = pltpu.SemaphoreType.DMA
    out_a, out_b = pl.pallas_call(
        functools.partial(kernel, n_row, n_col),
        out_shape=(
            jax.ShapeDtypeStruct((own_a, side, rank), f32),
            jax.ShapeDtypeStruct((own_b, side, rank), f32),
        ),
        in_specs=[smem, smem, vmem, vmem, vmem, pl.BlockSpec(memory_space=pl.ANY)],
        out_specs=(vmem, vmem),
        scratch_shapes=[
            pltpu.VMEM((slots, depth * side, side), jnp.int32),
            pltpu.VMEM((n_col, own_a, side, rank), f32),
            pltpu.VMEM((n_row, own_b, side, rank), f32),
            pltpu.VMEM((slots, side, rank), f32),
            pltpu.VMEM((slots, side, rank), f32),
            pltpu.VMEM((STEPS, n_col, slots, side, rank), f32),
            pltpu.VMEM((STEPS, n_row, slots, side, rank), f32),
            pltpu.VMEM((n_col, lines, rank), f32),
            pltpu.VMEM((n_row, lines, rank), f32),
            pltpu.VMEM((max(slots, own_a), side, rank), f32),
            pltpu.VMEM((max(slots, own_b), side, rank), f32),
            dma((slots,)),
            dma((STEPS, 2, n_col, slots)),
            dma((STEPS, n_col, slots)),
            dma((2, n_col, own_a)),
            dma((n_col, own_a)),
            dma((n_row - 1, own_b)),
            dma((n_row, own_b)),
            dma((STEPS, 2 * chips - 1, slots)),
            dma((STEPS, n_row, slots)),
            dma((n_col - 1,)),
            dma((n_col,)),
            dma((n_row - 1,)),
            dma((n_row,)),
        ],
        compiler_params=pltpu.CompilerParams(
            collective_id=0, has_side_effects=True, vmem_limit_bytes=56 * 1024 * 1024
        ),
    )(
        block_coords.reshape(3, slots),
        block_count,
        factor_a.reshape(own_a, side, rank),
        factor_b.reshape(own_b, side, rank),
        factor_c.reshape(-1, depth, rank),
        counts.reshape(slots, depth * side, side),
    )
    return out_a.reshape(factor_a.shape), out_b.reshape(factor_b.shape)


def solution(mesh):
    n_row = mesh.shape["row"]
    n_col = mesh.shape["col"]
    return jax.shard_map(
        functools.partial(local, n_row, n_col),
        mesh=mesh,
        in_specs=(
            P("row", "col", None, None, None, None),
            P(None, "row", "col", None),
            P("row", "col"),
            P(("row", "col"), None),
            P(("col", "row"), None),
            P(),
        ),
        out_specs=(P(("row", "col"), None), P(("col", "row"), None)),
        check_vma=False,
    )
```

time: 374 us -> 91 us (0.24)
  waiting for transfers between devices: 273 us -> 0 us
  Pallas kernels: 0 us -> 85 us
  loops' own time: 27.5 us -> 0 us
  local copies, waits for them, and re-layouts: 23.1 us -> 4.5 us
  matrix products: 18.2 us -> 0 us
  other arithmetic: 15.6 us -> 0 us
  between operations: 14.2 us -> 1.29 us
    reduce_scatter x4 -> x0, waiting for transfers between devices: 161 us -> none  [the longest x2 106 us: local(): share_b = lax.psum_scatter(grad_b, 'row', scatter_dimension=0, tiled=True)]
    all_gather x4 -> x0, waiting for transfers between devices: 109 us -> none  [the longest x2 61.6 us: local(): band_a = lax.all_gather(factor_a, 'col', axis=0, tiled=True)]
    pallas_call x0 -> x1, Pallas kernels: none -> 85 us  [local(): pl.pallas_call(functools.partial(kernel, n_row, n_col), out_shape=(jax.Sh...]
    another operation x2 -> x0, loops' own time: 27.5 us -> none  [local_gradients(): lax.fori_loop(0, limit, lambda slot_index, partial_value: visit_slot(part...]
    dynamic_slice x24 -> x0, local copies, waits for them, and re-layouts: 20.4 us -> none  [the longest x8 7.72 us: visit_slot(): start_b = block_coords[1, 0, 0, slot_index] * side]
    dot_general x24 -> x0, matrix products: 18.2 us -> none  [the longest x8 8.21 us: block_gradient(): jnp.dot(residual.T, scaled_a, precision=highest, preferred_element_type=j...]
    convert_element_type x8 -> x0, other arithmetic: 8.67 us -> none  [block_gradient(): observed.reshape(depth * side, side).astype(jnp.float32)]
    sub x4 -> x0, other arithmetic: 6.64 us -> none  [the longest x2 3.37 us: local(): factor_a = factor_a - step_rate * share_a]
  transfers between devices with their start and end apart: 8 -> 0, of which waited for: 8 -> 0; matrix products, arithmetic and copies ran while one was open for 1% -> 0% of each run, Pallas kernels for 0% -> 0%
where the time goes in v1:
time: 91 us; the launch traced here: 90.8 us
  Pallas kernels  85 us (93%)
  local copies, waits for them, and re-layouts  4.5 us (5%)
  between operations  1.29 us (1%)
    pallas_call x1, Pallas kernels, local(): pl.pallas_call(functools.partial(kernel, n_row, n_col), out_shape=(jax.Sh...  85 us
    unnamed x3, local copies, waits for them, and re-layouts  4.5 us

profile of v1, /device:TPU:0, one launch (start us, length us, event | category | flops | bytes accessed | tf_op | source)
XLA Modules:
  0.0 90.8 jit_solution(5485204668731224555)
XLA Ops:
  1.3 1.3 %copy.10 = s32[3,1,1,6]{3,0,1,2:T(4,128)} copy(s32[3,1,1,6]{3,2,1,0:T(1,128)} %param.7) | data formatting | bytes 144
  2.5 85.0 %shard_map.77 = (f32[4,128,128]{2,1,0:T(8,128)}, f32[2,128,128]{2,1,0:T(8,128)}) custom-call(s32[3,6]{1,0:T(4,128)} %bitcast.15, s32[1,1]{1,0:T(1,128)S(6)} %copy.13.limit_ref, f32[4,128,128]{2,1,0:T(8,128)} %bitcast.12, f32[2,128,128]{2,1,0:T(8,128)} %bitcast.13, f32[128,8,128]{2,1,0:T(8,128)} %bitcast.10, s32[6,1024,128]{2,1,0:T(8,128)} %bitcast.9), custom_call_target="tpu_custom_call" | custom-call | tf_op jit(solution)/shard_map/pallas_call | solution.py:321
  87.6 1.7 %copy.14 = f32[512,128]{1,0:T(8,128)} copy(f32[512,128]{1,0:T(8,128)} %bitcast.11) | data formatting | bytes 524288
  89.2 1.6 %copy.15 = f32[256,128]{1,0:T(8,128)} copy(f32[256,128]{1,0:T(8,128)} %bitcast.14) | data formatting | bytes 262144

commit v2 on v1

v2 whole, which is shorter than its diff:
```python
import functools

import jax
import jax.numpy as jnp
from jax import lax
from jax.experimental import pallas as pl
from jax.experimental.pallas import tpu as pltpu
from jax.sharding import PartitionSpec as P

STEPS = 2
SLICES = 8
step_rate = 0.004
MESH = pl.DeviceIdType.MESH


def split(x):
    high = x.astype(jnp.bfloat16)
    return high, (x - high.astype(jnp.float32)).astype(jnp.bfloat16)


def dot(x, y, dims):
    return lax.dot_general(x, y, (dims, ((), ())), preferred_element_type=jnp.float32)


def dot3(x, y, dims):
    return dot(x[0], y[0], dims) + (dot(x[0], y[1], dims) + dot(x[1], y[0], dims))


def kernel(n_row, n_col, coords, limit_ref, a_ref, b_ref, c_ref, counts_hbm, out_a, out_b,
           counts, band_a, band_b, sel_out, sel_in, cur_a, cur_b, raw_a, raw_b, part_out, part_in,
           tag_a, tag_b, acc_a, acc_b,
           counts_sem, ga_send, ga_recv, sel_send, sel_recv, gb_send, gb_recv,
           own_send, own_recv, far_send, far_recv, part_send, part_recv, rb_send, rb_recv, pb_send, pb_recv,
           ta_send, ta_recv, tb_send, tb_recv):
    r = lax.axis_index("row")
    c = lax.axis_index("col")
    own_a = a_ref.shape[0]
    own_b = b_ref.shape[0]
    side = a_ref.shape[1]
    slots = counts_hbm.shape[0]
    depth = c_ref.shape[1]
    chips = n_row // 2
    core = lax.rem(r, 2)
    partner = r + 1 - 2 * core
    limit = limit_ref[0, 0]
    end = n_col - 1
    both = jnp.logical_and
    high = side // SLICES
    groups = rb_recv.shape[2]
    bunch = slots // groups

    def loop(n, body):
        lax.fori_loop(0, n, lambda i, carry: (body(i), carry)[1], 0)

    def when(condition, body):
        pl.when(condition)(body)

    def row_peer(d):
        return lax.rem(r + d, n_row)

    def col_peer(d):
        return lax.rem(c + d, n_col)

    def chip_peer(d):
        return lax.rem(r + 2 * d, n_row)

    def cut(q):
        return pl.ds(pl.multiple_of(q * high, high), high)

    def remote(src, dst, send, recv, to):
        return pltpu.make_async_remote_copy(
            src_ref=src, dst_ref=dst, send_sem=send, recv_sem=recv, device_id=to, device_id_type=MESH)

    load_counts = [
        pltpu.make_async_copy(counts_hbm.at[s], counts.at[s], counts_sem.at[s]) for s in range(slots)
    ]
    for copy in load_counts:
        copy.start()

    barrier = pltpu.get_barrier_semaphore()
    loop(n_row - 1, lambda d: pl.semaphore_signal(
        barrier, inc=1, device_id=(row_peer(d + 1), c), device_id_type=MESH))
    loop(n_col - 1, lambda d: pl.semaphore_signal(
        barrier, inc=1, device_id=(r, col_peer(d + 1)), device_id_type=MESH))

    line = lax.broadcasted_iota(jnp.int32, tag_a.shape[1:], 0)
    mine_a = jnp.full(tag_a.shape[1:], -1.0, jnp.float32)
    mine_b = mine_a
    for s in range(slots):
        live = s < limit
        mine_a = jnp.where(line == s, jnp.where(live, coords[0, 0, 0, s], -1).astype(jnp.float32), mine_a)
        mine_b = jnp.where(line == s, jnp.where(live, coords[1, 0, 0, s], -1).astype(jnp.float32), mine_b)
    tag_a[c] = mine_a
    tag_b[r] = mine_b
    for p in range(own_a):
        band_a[c, p] = a_ref[p]
    for p in range(own_b):
        band_b[r, p] = b_ref[p]
    pl.semaphore_wait(barrier, n_row - 1 + n_col - 1)

    def tag_copy_a(o, d):
        return remote(tag_a.at[o], tag_a.at[o], ta_send.at[d - 1], ta_recv.at[o], (r, col_peer(d)))

    def tag_copy_b(o, d):
        return remote(tag_b.at[o], tag_b.at[o], tb_send.at[d - 1], tb_recv.at[o], (row_peer(d), c))

    def gather_b(o, d):
        return remote(band_b.at[o], band_b.at[o], gb_send.at[d - 1], gb_recv.at[o], (row_peer(d), c))

    loop(n_col - 1, lambda d: tag_copy_a(c, d + 1).start())

    def toward(k):
        return (r, c + 1 - 2 * k)

    def is_next_to_end(k):
        return c == n_col - 2 if k == 0 else c == 1

    def passes_rows(k):
        return c < n_col - 2 if k == 0 else c > 1

    def takes_rows(k):
        return c < end if k == 0 else c > 0

    def origin_of(k, d):
        return c - d if k == 0 else c + d

    def inside(o):
        return both(o >= 0, o < n_col)

    def gather_a(k, o, q):
        place = band_a.at[o, :, cut(q)]
        return remote(place, place, ga_send.at[k, o], ga_recv.at[o, q], toward(k))

    def choose(k, q):
        targets = tag_a[c + 1 - 2 * k]
        origins = range(0, n_col - 1) if k == 0 else range(1, n_col)
        for s in range(slots):
            target = targets[s:s + 1, :]
            total = jnp.zeros((high, a_ref.shape[2]), jnp.float32)
            for o in origins:
                for p in range(own_a):
                    total = jnp.where(target == float(o * own_a + p), band_a[o, p, cut(q)], total)
            sel_out[k, s, cut(q)] = total

    def sel_copy(k, q):
        return remote(sel_out.at[k, :, cut(q)], sel_in.at[:, cut(q)], sel_send.at[k], sel_recv.at[0], toward(k))

    def gather_slice(q):
        for k in range(2):
            when(passes_rows(k), lambda: gather_a(k, c, q).start())
        for d in range(1, n_col - 1):
            for k in range(2):
                o = origin_of(k, d)

                def arrived():
                    gather_a(k, o, q).wait_recv()
                    when(passes_rows(k), lambda: gather_a(k, o, q).start())

                when(both(inside(o), takes_rows(k)), arrived)
        for k in range(2):
            def chosen():
                when(q == 0, lambda: tag_copy_a(c + 1 - 2 * k, 1).wait_recv())
                choose(k, q)
                sel_copy(k, q).start()

            when(is_next_to_end(k), chosen)

    loop(n_row - 1, lambda d: gather_b(r, d + 1).start())
    loop(n_row - 1, lambda d: tag_copy_b(r, d + 1).start())
    loop(SLICES, gather_slice)

    def receive_tag(d):
        o = col_peer(d + 1)
        taken = jnp.logical_or(
            both(is_next_to_end(0), o == c + 1), both(is_next_to_end(1), o == c - 1))
        when(jnp.logical_not(taken), lambda: tag_copy_a(o, 1).wait_recv())

    loop(n_col - 1, receive_tag)
    loop(n_row - 1, lambda d: gather_b(row_peer(d + 1), 1).wait_recv())
    loop(n_row - 1, lambda d: tag_copy_b(row_peer(d + 1), 1).wait_recv())
    at_end = jnp.logical_or(c == 0, c == end)
    when(at_end, lambda: remote(sel_in, sel_in, sel_send.at[0], sel_recv.at[0], (r, c)).wait_recv())

    def first_pieces(s):
        ia = coords[0, 0, 0, s]
        ib = coords[1, 0, 0, s]
        cur_b[s] = band_b[ib // own_b, ib % own_b]

        def from_selection():
            cur_a[s] = jnp.where(ia // own_a == c, a_ref[ia % own_a], sel_in[s])

        def from_band():
            cur_a[s] = band_a[ia // own_a, ia % own_a]

        when(at_end, from_selection)
        when(jnp.logical_not(at_end), from_band)

    loop(slots, first_pieces)

    def gradients(t, s):
        piece_a = cur_a[s]
        piece_b = cur_b[s]
        piece_c = c_ref[coords[2, 0, 0, s]]
        flag = jnp.where(s < limit, 1.0, 0.0).astype(jnp.float32)
        scaled = (piece_c[:, None, :] * piece_a[None, :, :]).reshape(depth * side, -1)
        scaled = split(scaled)
        split_b = split(piece_b)
        model = dot3(scaled, split_b, ((1,), (1,)))
        observed = counts[s].astype(jnp.float32)
        residual = split((jnp.exp(model) - observed) * flag)
        product = dot3(residual, split_b, ((1,), (0,)))
        grad_a = jnp.sum(product.reshape(depth, side, -1) * piece_c[:, None, :], axis=0)
        grad_b = dot3(residual, scaled, ((0,), (0,)))
        if t:
            grad_a = grad_a + raw_a[t - 1, c, s]
            grad_b = grad_b + raw_b[t - 1, r, s]
        raw_a[t, c, s] = grad_a
        raw_b[t, r, s] = grad_b

    def absorb(raw, tag, acc, ids, t, o):
        tags = tag[o]
        for i, block in enumerate(ids):
            match = [tags[s:s + 1, :] == block for s in range(slots)]
            total = acc[i]
            for s in range(slots):
                total = total + jnp.where(match[s], raw[t, o, s], 0.0)
            acc[i] = total

    def own_copy(t, k, o, s):
        place = raw_a.at[t, o, s]
        return remote(place, place, own_send.at[t, k], own_recv.at[t, k], toward(k))

    def own_whole(t, k, o):
        place = raw_a.at[t, o]
        return remote(place, place, own_send.at[t, k], own_recv.at[t, k], toward(k))

    def far_copy(t, k, o, q):
        place = raw_a.at[t, o, :, cut(q)]
        return remote(place, place, far_send.at[t, k, o], far_recv.at[t, o, q], toward(k))

    def wanted(t):
        return own_a if t == STEPS - 1 else slots

    def part_copy(t, k, q):
        n = wanted(t)
        return remote(part_out.at[t, k, pl.ds(0, n), cut(q)], part_in.at[t, pl.ds(0, n), cut(q)],
                      part_send.at[t, k], part_recv.at[t], toward(k))

    def part_whole(t, k):
        n = wanted(t)
        return remote(part_out.at[t, k, pl.ds(0, n)], part_in.at[t, pl.ds(0, n)],
                      part_send.at[t, k], part_recv.at[t], toward(k))

    def bunch_b(t, o, g, to, send, recv):
        place = raw_b.at[t, o, pl.ds(g * bunch, bunch)]
        return remote(place, place, send, recv, (to, c))

    def cross_send(t, s, d):
        g = s // bunch
        place = raw_b.at[t, r, s]
        return remote(place, place, rb_send.at[t, d - 1], rb_recv.at[t, r, g], (chip_peer(d), c))

    def cross_recv(t, o, g):
        return bunch_b(t, o, g, r, rb_send.at[t, 0], rb_recv.at[t, o, g])

    def pair_send(t, s):
        place = raw_b.at[t, r, s]
        return remote(place, place, pb_send.at[t, 0], pb_recv.at[t, r, s // bunch], (partner, c))

    def pair_pass(t, d, g):
        o = chip_peer(d)
        return bunch_b(t, o, g, partner, pb_send.at[t, d], pb_recv.at[t, o, g])

    def pair_recv(t, o, g):
        return bunch_b(t, o, g, r, pb_send.at[t, 0], pb_recv.at[t, o, g])

    def step(t):
        last = t == STEPS - 1

        def one(s):
            for k in range(slots):
                if t == 0:
                    when(s == k, load_counts[k].wait)
            gradients(t, s)
            when(c < end, lambda: own_copy(t, 0, c, s).start())
            when(c > 0, lambda: own_copy(t, 1, c, s).start())
            loop(chips - 1, lambda d: cross_send(t, s, d + 1).start())
            pair_send(t, s).start()

        loop(slots, one)
        if last:
            ids_a = [(c * own_a + p).astype(jnp.float32) for p in range(own_a)]
            ids_b = [(r * own_b + p).astype(jnp.float32) for p in range(own_b)]
        else:
            ids_a = [coords[0, 0, 0, s].astype(jnp.float32) for s in range(slots)]
            ids_b = [coords[1, 0, 0, s].astype(jnp.float32) for s in range(slots)]
        take_a = lambda o: absorb(raw_a, tag_a, acc_a, ids_a, t, o)
        take_b = lambda o: absorb(raw_b, tag_b, acc_b, ids_b, t, o)
        acc_a[...] = jnp.zeros_like(acc_a)
        acc_b[...] = jnp.zeros_like(acc_b)
        take_a(c)
        take_b(r)

        for k in range(2):
            o = origin_of(k, 1)

            def neighbour():
                own_whole(t, k, o).wait_recv()
                when(passes_rows(k), lambda: loop(SLICES, lambda q: far_copy(t, k, o, q).start()))

            when(inside(o), neighbour)
        for g in range(groups):
            pair_recv(t, partner, g).wait_recv()

        def part(k, q):
            there = c + 1 - 2 * k
            origins = range(0, n_col - 2) if k == 0 else range(2, n_col)
            aims = tag_a[there]
            for i in range(wanted(t)):
                if last:
                    aim = (there * own_a + i).astype(jnp.float32)
                else:
                    aim = aims[i:i + 1, :]
                total = jnp.zeros((high, a_ref.shape[2]), jnp.float32)
                for o in origins:
                    tags = tag_a[o]
                    for s in range(slots):
                        total = total + jnp.where(tags[s:s + 1, :] == aim, raw_a[t, o, s, cut(q)], 0.0)
                part_out[t, k, i, cut(q)] = total

        def far_slice(q):
            for d in range(2, n_col - 1):
                for k in range(2):
                    o = origin_of(k, d)

                    def arrived():
                        far_copy(t, k, o, q).wait_recv()
                        when(passes_rows(k), lambda: far_copy(t, k, o, q).start())

                    when(both(inside(o), takes_rows(k)), arrived)
            if n_col > 2:
                for k in range(2):
                    def summed():
                        part(k, q)
                        part_copy(t, k, q).start()

                    when(is_next_to_end(k), summed)

        loop(SLICES, far_slice)
        take_b(partner)
        for k in range(2):
            when(inside(origin_of(k, 1)), lambda: take_a(origin_of(k, 1)))

        def hand_over(d):
            for g in range(groups):
                cross_recv(t, chip_peer(d), g).wait_recv()
                pair_pass(t, d, g).start()

        loop(chips - 1, lambda d: hand_over(d + 1))
        loop(chips - 1, lambda d: take_b(chip_peer(d + 1)))

        def far_take(d):
            for k in range(2):
                o = origin_of(k, d)
                when(both(inside(o), takes_rows(k)), lambda: take_a(o))

        loop(max(n_col - 3, 0), lambda d: far_take(d + 2))
        if n_col > 2:
            def add_part():
                part_whole(t, 0).wait_recv()
                for i in range(wanted(t)):
                    acc_a[i] = acc_a[i] + part_in[t, i]

            when(at_end, add_part)

        def receive_pair(d):
            o = lax.rem(partner + 2 * d, n_row)
            for g in range(groups):
                pair_recv(t, o, g).wait_recv()
            take_b(o)

        loop(chips - 1, lambda d: receive_pair(d + 1))
        if last:
            for p in range(own_a):
                out_a[p] = a_ref[p] - step_rate * acc_a[p]
            for p in range(own_b):
                out_b[p] = b_ref[p] - step_rate * acc_b[p]
        else:
            for s in range(slots):
                cur_a[s] = cur_a[s] - step_rate * acc_a[s]
                cur_b[s] = cur_b[s] - step_rate * acc_b[s]

    for t in range(STEPS):
        step(t)

    for k in range(2):
        def sent_shard(o, k=k):
            place = band_a.at[o]
            remote(place, place, ga_send.at[k, o], ga_recv.at[o, 0], toward(k)).wait_send()

        def sent_far(t, o, k=k):
            place = raw_a.at[t, o]
            remote(place, place, far_send.at[t, k, o], far_recv.at[t, o, 0], toward(k)).wait_send()

        def sent_from(d):
            o = origin_of(k, d)
            when(both(inside(o), passes_rows(k)), lambda: sent_shard(o))

        def sent_far_from(d):
            o = origin_of(k, d)
            for t in range(STEPS):
                when(both(inside(o), passes_rows(k)), lambda: sent_far(t, o))

        loop(n_col - 1, sent_from)
        loop(n_col - 2, lambda d: sent_far_from(d + 1))
        when(is_next_to_end(k),
             lambda: remote(sel_out.at[k], sel_in, sel_send.at[k], sel_recv.at[0], toward(k)).wait_send())
        for t in range(STEPS):
            when(c < end if k == 0 else c > 0, lambda: own_whole(t, k, c).wait_send())
            if n_col > 2:
                when(is_next_to_end(k), lambda: part_whole(t, k).wait_send())
    loop(n_row - 1, lambda d: gather_b(r, d + 1).wait_send())
    loop(n_col - 1, lambda d: tag_copy_a(c, d + 1).wait_send())
    loop(n_row - 1, lambda d: tag_copy_b(r, d + 1).wait_send())
    for t in range(STEPS):
        place = raw_b.at[t, r]
        loop(chips - 1, lambda d: remote(
            place, place, rb_send.at[t, d], rb_recv.at[t, r, 0], (chip_peer(d + 1), c)).wait_send())
        loop(chips, lambda d: remote(
            place, place, pb_send.at[t, d], pb_recv.at[t, r, 0], (partner, c)).wait_send())


def local(n_row, n_col, counts, block_coords, block_count, factor_a, factor_b, factor_c):
    slots, depth, side = counts.shape[2:5]
    rank = factor_a.shape[1]
    own_a = factor_a.shape[0] // side
    own_b = factor_b.shape[0] // side
    chips = n_row // 2
    lines = -(-slots // 8) * 8
    groups = 2 if slots % 2 == 0 else 1
    most = max(slots, own_a)
    f32 = jnp.float32
    vmem = pl.BlockSpec(memory_space=pltpu.VMEM)
    smem = pl.BlockSpec(memory_space=pltpu.SMEM)
    dma = pltpu.SemaphoreType.DMA
    out_a, out_b = pl.pallas_call(
        functools.partial(kernel, n_row, n_col),
        out_shape=(
            jax.ShapeDtypeStruct((own_a, side, rank), f32),
            jax.ShapeDtypeStruct((own_b, side, rank), f32),
        ),
        in_specs=[smem, smem, vmem, vmem, vmem, pl.BlockSpec(memory_space=pl.ANY)],
        out_specs=(vmem, vmem),
        scratch_shapes=[
            pltpu.VMEM((slots, depth * side, side), jnp.int32),
            pltpu.VMEM((n_col, own_a, side, rank), f32),
            pltpu.VMEM((n_row, own_b, side, rank), f32),
            pltpu.VMEM((2, slots, side, rank), f32),
            pltpu.VMEM((slots, side, rank), f32),
            pltpu.VMEM((slots, side, rank), f32),
            pltpu.VMEM((slots, side, rank), f32),
            pltpu.VMEM((STEPS, n_col, slots, side, rank), f32),
            pltpu.VMEM((STEPS, n_row, slots, side, rank), f32),
            pltpu.VMEM((STEPS, 2, most, side, rank), f32),
            pltpu.VMEM((STEPS, most, side, rank), f32),
            pltpu.VMEM((n_col, lines, rank), f32),
            pltpu.VMEM((n_row, lines, rank), f32),
            pltpu.VMEM((most, side, rank), f32),
            pltpu.VMEM((max(slots, own_b), side, rank), f32),
            dma((slots,)),
            dma((2, n_col)),
            dma((n_col, SLICES)),
            dma((2,)),
            dma((1,)),
            dma((n_row - 1,)),
            dma((n_row,)),
            dma((STEPS, 2)),
            dma((STEPS, 2)),
            dma((STEPS, 2, n_col)),
            dma((STEPS, n_col, SLICES)),
            dma((STEPS, 2)),
            dma((STEPS,)),
            dma((STEPS, chips - 1)),
            dma((STEPS, n_row, groups)),
            dma((STEPS, chips)),
            dma((STEPS, n_row, groups)),
            dma((n_col - 1,)),
            dma((n_col,)),
            dma((n_row - 1,)),
            dma((n_row,)),
        ],
        compiler_params=pltpu.CompilerParams(
            collective_id=0, has_side_effects=True, vmem_limit_bytes=56 * 1024 * 1024
        ),
    )(
        block_coords,
        block_count,
        factor_a.reshape(own_a, side, rank),
        factor_b.reshape(own_b, side, rank),
        factor_c.reshape(-1, depth, rank),
        counts.reshape(slots, depth * side, side),
    )
    return out_a.reshape(factor_a.shape), out_b.reshape(factor_b.shape)


def solution(mesh):
    n_row = mesh.shape["row"]
    n_col = mesh.shape["col"]
    return jax.shard_map(
        functools.partial(local, n_row, n_col),
        mesh=mesh,
        in_specs=(
            P("row", "col", None, None, None, None),
            P(None, "row", "col", None),
            P("row", "col"),
            P(("row", "col"), None),
            P(("col", "row"), None),
            P(),
        ),
        out_specs=(P(("row", "col"), None), P(("col", "row"), None)),
        check_vma=False,
    )
```

time: 91 us -> 111 us (1.22)
  Pallas kernels: 85 us -> 106 us
  local copies, waits for them, and re-layouts: 4.5 us -> 3.24 us
    pallas_call x1, Pallas kernels: 85 us -> 106 us  [local(): pl.pallas_call(functools.partial(kernel, n_row, n_col), out_shape=(jax.Sh...]
    unnamed x3 -> x2, local copies, waits for them, and re-layouts: 4.5 us -> 3.24 us
where the time goes in v2:
time: 111 us
  Pallas kernels  106 us (95%)
  local copies, waits for them, and re-layouts  3.24 us (3%)
  between operations  1.28 us (1%)
    pallas_call x1, Pallas kernels, local(): pl.pallas_call(functools.partial(kernel, n_row, n_col), out_shape=(jax.Sh...  106 us
    unnamed x2, local copies, waits for them, and re-layouts  3.24 us

profile of v2, /device:TPU:0, one launch (start us, length us, event | category | flops | bytes accessed | tf_op | source)
XLA Modules:
  0.0 110.8 jit_solution(15035630586393275979)
XLA Ops:
  1.3 106.3 %shard_map.77 = (f32[4,128,128]{2,1,0:T(8,128)}, f32[2,128,128]{2,1,0:T(8,128)}) custom-call(s32[3,1,1,6]{3,2,1,0:T(1,128)} %coords.1, s32[1,1]{1,0:T(1,128)S(6)} %copy.10.limit_ref, f32[4,128,128]{2,1,0:T(8,128)} %bitcast.8, f32[2,128,128]{2,1,0:T(8,128)} %bitcast.10, f32[128,8,128]{2,1,0:T(8,128)} %bitcast.7, s32[6,1024,128]{2,1,0:T(8,128)} %bitcast.6), custom_call_target="tpu_custom_call" | custom-call | tf_op jit(solution)/shard_map/pallas_call | solution.py:446
  107.5 1.7 %copy.11 = f32[512,128]{1,0:T(8,128)} copy(f32[512,128]{1,0:T(8,128)} %bitcast.9) | data formatting | bytes 524288
  109.2 1.6 %copy.12 = f32[256,128]{1,0:T(8,128)} copy(f32[256,128]{1,0:T(8,128)} %bitcast.11) | data formatting | bytes 262144

commit v3 on v2

--- a/solution.py
+++ b/solution.py
@@ -8,7 +8,7 @@
 from jax.sharding import PartitionSpec as P
 
 STEPS = 2
-SLICES = 8
+SLICES = 2
 step_rate = 0.004
 MESH = pl.DeviceIdType.MESH
 

time: 111 us -> 85.6 us (0.77)
  Pallas kernels: 106 us -> 80.9 us
    pallas_call x1, Pallas kernels: 106 us -> 80.9 us  [local(): pl.pallas_call(functools.partial(kernel, n_row, n_col), out_shape=(jax.Sh...]
where the time goes in v3:
time: 85.6 us; the launch traced here: 85.4 us
  Pallas kernels  80.9 us (95%)
  local copies, waits for them, and re-layouts  3.24 us (4%)
  between operations  1.28 us (1%)
    pallas_call x1, Pallas kernels, local(): pl.pallas_call(functools.partial(kernel, n_row, n_col), out_shape=(jax.Sh...  80.9 us
    unnamed x2, local copies, waits for them, and re-layouts  3.24 us

profile of v3, /device:TPU:0, one launch (start us, length us, event | category | flops | bytes accessed | tf_op | source)
XLA Modules:
  0.0 85.4 jit_solution(4382722306133977224)
XLA Ops:
  1.3 80.9 %shard_map.77 = (f32[4,128,128]{2,1,0:T(8,128)}, f32[2,128,128]{2,1,0:T(8,128)}) custom-call(s32[3,1,1,6]{3,2,1,0:T(1,128)} %coords.1, s32[1,1]{1,0:T(1,128)S(6)} %copy.10.limit_ref, f32[4,128,128]{2,1,0:T(8,128)} %bitcast.8, f32[2,128,128]{2,1,0:T(8,128)} %bitcast.10, f32[128,8,128]{2,1,0:T(8,128)} %bitcast.7, s32[6,1024,128]{2,1,0:T(8,128)} %bitcast.6), custom_call_target="tpu_custom_call" | custom-call | tf_op jit(solution)/shard_map/pallas_call | solution.py:446
  82.1 1.7 %copy.11 = f32[512,128]{1,0:T(8,128)} copy(f32[512,128]{1,0:T(8,128)} %bitcast.9) | data formatting | bytes 524288
  83.8 1.6 %copy.12 = f32[256,128]{1,0:T(8,128)} copy(f32[256,128]{1,0:T(8,128)} %bitcast.11) | data formatting | bytes 262144
